TPU v7x, 32 devices: a whole 2x2x4 slice. The times are simulated.
32 devices in a mesh: group: 2 (over x), tm: 16 (over z, y, core).
Axes of the slice: x: 2, y: 2, z: 4, core: 2. Of those that a mesh axis runs over, the one named last changes fastest.
Arguments:
- patches: bfloat16 [32, 1024, 128], P(('group', 'tm')), parts along dimension 0, may hold values from -6 to 6
- classes: int32 [32], P(('group', 'tm')), parts along dimension 0, may hold values from 0 to 15
- dilations: int32 [4], replicated, may hold values from 1 to 4, as said below
- enc_weight: bfloat16 [128, 256], replicated, may hold values from -0.5 to 0.5
- cond_table: bfloat16 [16, 256], replicated, may hold values from -3 to 3
- temp_weight: bfloat16 [4, 512, 256], replicated, may hold values from -0.25 to 0.25
- dec_weight: bfloat16 [256, 128], replicated, may hold values from -0.375 to 0.375
- cotangent: bfloat16 [32, 1024, 128], P(('group', 'tm')), parts along dimension 0, may hold values from -0.125 to 0.125
Outputs:
- decoded: bfloat16 [32, 1024, 128], P(('group', 'tm')), parts along dimension 0
- grad_encoder: float32 [256, 256], P(('group', 'tm')), parts along dimension 0
- grad_temporal: float32 [8, 512, 256], P('group', 'tm'), parts along dimension 0
- grad_decoder: float32 [512, 128], P(('group', 'tm')), parts along dimension 0
There are 2 independent parts, one for each index of `group`. A program takes and returns all parts, laid end to end along the dimension named above; an argument that names none is the same for every part. Nothing has to cross between parts.
Inputs may be any that keep to these rules, and one draw needn't show every extreme that they name: `dilations`: every layer's dilation lies in 1 to 4, and some layer's is exactly 4.
All inputs are finite; a program needn't handle non-finite values.
Results may differ from a plain program's by a relative error of at most 0.009.
Values may be sent and summed in bfloat16 or wider, within the bound.
A program may use at most 64 MiB of HBM per device.

v0:
```python
import jax
import jax.numpy as jnp
from jax import lax
from jax.sharding import PartitionSpec as P


def shift_late(values, spacing, margin):
    filler = jnp.zeros((margin,) + values.shape[1:], values.dtype)
    padded = jnp.concatenate([filler, values], axis=0)
    return lax.dynamic_slice_in_dim(padded, margin - spacing, values.shape[0], 0)


def shift_early(values, spacing, margin):
    filler = jnp.zeros((margin,) + values.shape[1:], values.dtype)
    padded = jnp.concatenate([values, filler], axis=0)
    return lax.dynamic_slice_in_dim(padded, spacing, values.shape[0], 0)


def encode_rows(patch_rows, frame_kinds, enc_weight, cond_table):
    kinds = cond_table.shape[0]
    onehot = (frame_kinds[:, None] == jnp.arange(kinds, dtype=jnp.int32)[None, :]).astype(
        jnp.bfloat16
    )
    embedded = jnp.dot(onehot, cond_table, preferred_element_type=jnp.float32)
    start = jnp.einsum("tpc,cd->tpd", patch_rows, enc_weight, preferred_element_type=jnp.float32)
    return (start + embedded[:, None, :]).astype(jnp.bfloat16)


def shards(patches, classes, dilations, enc_weight, cond_table, temp_weight, dec_weight, cotangent):
    layers = temp_weight.shape[0]
    width = temp_weight.shape[2]
    start = encode_rows(patches, classes, enc_weight, cond_table)
    latent = lax.all_to_all(start, "tm", split_axis=1, concat_axis=0, tiled=True)
    margin = latent.shape[0] // 4
    saved = []
    for layer in range(layers):
        joined = jnp.concatenate([latent, shift_late(latent, dilations[layer], margin)], axis=-1)
        pre_act = jnp.einsum(
            "tpk,kd->tpd", joined, temp_weight[layer], preferred_element_type=jnp.float32
        )
        saved.append((joined, pre_act))
        latent = (latent.astype(jnp.float32) + jax.nn.silu(pre_act)).astype(jnp.bfloat16)
    final = lax.all_to_all(latent, "tm", split_axis=0, concat_axis=1, tiled=True)
    decoded = jnp.einsum(
        "fpd,dc->fpc", final, dec_weight, preferred_element_type=jnp.float32
    ).astype(jnp.bfloat16)
    dec_term = jnp.einsum("fpd,fpc->dc", final, cotangent, preferred_element_type=jnp.float32)
    upstream = jnp.einsum(
        "fpc,dc->fpd", cotangent, dec_weight, preferred_element_type=jnp.float32
    ).astype(jnp.bfloat16)
    carried = lax.all_to_all(upstream, "tm", split_axis=1, concat_axis=0, tiled=True)
    layer_terms = [None] * layers
    for layer in reversed(range(layers)):
        joined, pre_act = saved[layer]
        gate_value = jax.nn.sigmoid(pre_act)
        dpre = (
            carried.astype(jnp.float32) * gate_value * (1.0 + pre_act * (1.0 - gate_value))
        ).astype(jnp.bfloat16)
        layer_term = jnp.einsum("tpk,tpd->kd", joined, dpre, preferred_element_type=jnp.float32)
        layer_terms[layer] = layer_term
        returned = jnp.einsum(
            "tpd,kd->tpk", dpre, temp_weight[layer], preferred_element_type=jnp.float32
        )
        carried = (
            carried.astype(jnp.float32)
            + returned[..., :width]
            + shift_early(returned[..., width:], dilations[layer], margin)
        ).astype(jnp.bfloat16)
    stacked = jnp.stack(layer_terms)
    grad_temporal = lax.psum_scatter(stacked, "tm", scatter_dimension=1, tiled=True)
    carried_frames = lax.all_to_all(carried, "tm", split_axis=0, concat_axis=1, tiled=True)
    enc_term = jnp.einsum(
        "fpc,fpd->cd", patches, carried_frames, preferred_element_type=jnp.float32
    )
    grad_encoder, grad_decoder = (
        lax.psum_scatter(enc_term, "tm", scatter_dimension=0, tiled=True),
        lax.psum_scatter(dec_term, "tm", scatter_dimension=0, tiled=True),
    )
    return (decoded, grad_encoder, grad_temporal, grad_decoder)


def solution(mesh):
    in_specs = (
        P(("group", "tm"), None, None),
        P(("group", "tm")),
        P(),
        P(),
        P(),
        P(),
        P(),
        P(("group", "tm"), None, None),
    )
    out_specs = (
        P(("group", "tm"), None, None),
        P(("group", "tm"), None),
        P("group", "tm", None),
        P(("group", "tm"), None),
    )
    return jax.shard_map(shards, mesh=mesh, in_specs=in_specs, out_specs=out_specs, check_vma=False)
```

profile of v0, /device:TPU:0, one launch (start us, length us, event | category | flops | bytes accessed | tf_op | source)
XLA Modules:
  0.0 280.7 jit_solution(17788033939454266709)
XLA Ops:
  7.9 0.8 fusion.47
  8.7 1.2 fusion.2
  9.9 0.8 copy.26
  10.7 0.5 broadcast.31
  11.3 3.8 %reduce.1 = bf16[1024,256]{1,0:T(8,128)(2,1)S(1)} reduce(bf16[1024,1,256]{2,1,0:T(2,128)(2,1)S(1)} %bitcast.97, bf16[]{:T(256)} %broadcast.31), dimensions={1}, to_apply=%bitcast.92.reduce_sub_computation | reduce | bytes 1048578
  15.1 0.9 reshape.78
  16.0 7.4 %all-to-all-start = ((bf16[16,2,8192]{2,1,0:T(2,128)(2,1)}), bf16[16,2,8192]{2,1,0:T(2,128)(2,1)S(1)}, u32[]{:S(2)}, u32[]{:S(2)}) async-start(bf16[16,2,8192]{2,1,0:T(2,128)(2,1)} %reshape.78), calls=%async_computation | async-start | bytes 1048576 | tf_op jit(solution)/shard_map/all_to_all | solution.py:33
  23.5 0.3 fusion.1
  23.8 0.8 copy.25
  24.6 3.8 %reduce = bf16[1024,256]{1,0:T(8,128)(2,1)S(1)} reduce(bf16[1024,1,256]{2,1,0:T(2,128)(2,1)S(1)} %bitcast.98, bf16[]{:T(256)} %broadcast.31), dimensions={1}, to_apply=%bitcast.91.reduce_sub_computation | reduce | bytes 1048578
  28.4 0.9 reshape.76
  29.4 8.5 %all-to-all-done = bf16[16,2,8192]{2,1,0:T(2,128)(2,1)S(1)} async-done(((bf16[16,2,8192]{2,1,0:T(2,128)(2,1)}), bf16[16,2,8192]{2,1,0:T(2,128)(2,1)S(1)}, u32[]{:S(2)}, u32[]{:S(2)}) %all-to-all-start) | async-done | bytes 524320 | tf_op jit(solution)/shard_map/all_to_all | solution.py:33
  37.9 4.1 %all-to-all-start.2 = ((bf16[16,2,8192]{2,1,0:T(2,128)(2,1)}), bf16[16,2,8192]{2,1,0:T(2,128)(2,1)S(1)}, u32[]{:S(2)}, u32[]{:S(2)}) async-start(bf16[16,2,8192]{2,1,0:T(2,128)(2,1)} %reshape.76), calls=%async_computation.2 | async-start | bytes 1048576 | tf_op jit(solution)/shard_map/all_to_all | solution.py:51
  42.0 0.6 fusion.66
  55.6 0.5 reshape.79
  56.5 0.5 reshape.77
  57.2 2.6 add_convert_fusion.3
  59.9 1.4 add_convert_fusion.2
  61.4 1.4 add_convert_fusion.1
  62.9 1.5 multiply_convert_fusion
  64.4 5.7 %all-to-all-start.1 = ((bf16[16,64,256]{2,1,0:T(8,128)(2,1)}), bf16[16,64,256]{2,1,0:T(8,128)(2,1)S(1)}, u32[]{:S(2)}, u32[]{:S(2)}) async-start(bf16[16,64,256]{2,1,0:T(8,128)(2,1)} %get-tuple-element.17), calls=%async_computation.1 | async-start | bytes 1048576 | tf_op jit(solution)/shard_map/all_to_all | solution.py:43
  70.1 1.4 fusion.25
  71.7 0.3 fusion.5
  72.0 0.9 copy-done.19
  72.9 0.3 copy-done.24
  73.2 0.6 fusion.28
  74.2 0.9 copy-done.23
  75.2 0.6 fusion.31
  75.9 0.3 fusion.9
  76.2 0.9 copy-done.21
  77.2 0.6 fusion.34
  77.9 1.1 fusion.11
  79.1 1.5 convolution_bitcast_fusion.1
  80.6 4.0 %all-to-all-done.1 = bf16[16,64,256]{2,1,0:T(8,128)(2,1)S(1)} async-done(((bf16[16,64,256]{2,1,0:T(8,128)(2,1)}), bf16[16,64,256]{2,1,0:T(8,128)(2,1)S(1)}, u32[]{:S(2)}, u32[]{:S(2)}) %all-to-all-start.1) | async-done | bytes 524320 | tf_op jit(solution)/shard_map/all_to_all | solution.py:43
  84.6 4.1 %all-to-all-start.3 = ((bf16[16,64,256]{2,1,0:T(8,128)(2,1)}), bf16[16,64,256]{2,1,0:T(8,128)(2,1)S(1)}, u32[]{:S(2)}, u32[]{:S(2)}) async-start(bf16[16,64,256]{2,1,0:T(8,128)(2,1)} %fusion.11), calls=%async_computation.3 | async-start | bytes 1048576 | tf_op jit(solution)/shard_map/all_to_all | solution.py:71
  88.8 3.1 %convolution_bitcast_fusion.2 = f32[1,512,256]{2,1,0:T(8,128)} fusion(bf16[16,64,256]{2,1,0:T(8,128)(2,1)} %copy-done.7, bf16[16,64,256]{2,1,0:T(8,128)(2,1)} %copy-done.6, bf16[16,64,256]{2,1,0:T(8,128)(2,1)S(1)} %fusion.7, f32[16,64,256]{2,1,0:T(8,128)} %get-tuple-element.25), kind=kOutput, calls=%fused_computation.18 | convolution fusion | flops 273154048 | bytes 3145728 | tf_op jit(solution)/shard_map/tpk,tpd->kd/dot_general | solution.py:59
  91.9 1.5 convolution_bitcast_fusion.3
  93.4 1.0 fusion.22
  94.5 8.7 %all-to-all-done.3 = bf16[16,64,256]{2,1,0:T(8,128)(2,1)S(1)} async-done(((bf16[16,64,256]{2,1,0:T(8,128)(2,1)}), bf16[16,64,256]{2,1,0:T(8,128)(2,1)S(1)}, u32[]{:S(2)}, u32[]{:S(2)}) %all-to-all-start.3) | async-done | bytes 524320 | tf_op jit(solution)/shard_map/all_to_all | solution.py:71
  103.2 0.3 convolution_bitcast_fusion.4
  103.5 0.8 copy.19
  104.4 0.5 convolution_bitcast_fusion
  104.9 0.5 copy-done.14
  105.7 1.5 pad_maximum_fusion
  107.2 1.0 fusion.3
  108.2 42.8 %reduce-scatter.8.cloned.1.call-done = f32[16,128]{1,0:T(8,128)} async-done(((f32[256,128]{1,0:T(8,128)}), f32[16,128]{1,0:T(8,128)}) %reduce-scatter.8.cloned.1.call-update) | async-done | bytes 8208 | tf_op jit(solution)/shard_map/reduce_scatter | solution.py:77
  151.0 58.2 %reduce-scatter.10.cloned.1.call-done = f32[8,256]{1,0:T(8,128)} async-done(((f32[128,256]{1,0:T(8,128)}), f32[8,256]{1,0:T(8,128)}) %reduce-scatter.10.cloned.1.call-update) | async-done | bytes 8208
  209.2 65.0 %reduce-scatter.6.cloned.1.call-done = f32[4,32,256]{2,1,0:T(8,128)} async-done(((f32[4,512,256]{2,1,0:T(8,128)}), f32[4,32,256]{2,1,0:T(8,128)}) %reduce-scatter.6.cloned.1.call-update) | async-done | bytes 131088 | tf_op jit(solution)/shard_map/reduce_scatter | solution.py:70
  (63 shorter events, 2.1 us)
Async XLA Ops:
  7.2 16.3 %copy-start = (bf16[1,1024,128]{2,1,0:T(8,128)(2,1)S(1)}, bf16[1,1024,128]{2,1,0:T(8,128)(2,1)}, u32[]{:S(2)}) copy-start(bf16[1,1024,128]{2,1,0:T(8,128)(2,1)} %param.15) | copy-start | bytes 786436
  10.7 12.7 %copy-start.17 = (bf16[256,128]{1,0:T(8,128)(2,1)S(1)}, bf16[256,128]{1,0:T(8,128)(2,1)}, u32[]{:S(2)}) copy-start(bf16[256,128]{1,0:T(8,128)(2,1)} %param.14) | copy-start | bytes 196612
  16.0 21.9 %all-to-all-start = ((bf16[16,2,8192]{2,1,0:T(2,128)(2,1)}), bf16[16,2,8192]{2,1,0:T(2,128)(2,1)S(1)}, u32[]{:S(2)}, u32[]{:S(2)}) async-start(bf16[16,2,8192]{2,1,0:T(2,128)(2,1)} %reshape.78), calls=%async_computation | async-start | bytes 1048576 | tf_op jit(solution)/shard_map/all_to_all | solution.py:33
  24.6 17.4 %copy-start.20 = (s32[4]{0:T(128)S(1)}, s32[4]{0:T(128)}, u32[]{:S(2)}) copy-start(s32[4]{0:T(128)} %param.10) | copy-start | bytes 52
  37.9 18.6 %all-to-all-start.2 = ((bf16[16,2,8192]{2,1,0:T(2,128)(2,1)}), bf16[16,2,8192]{2,1,0:T(2,128)(2,1)S(1)}, u32[]{:S(2)}, u32[]{:S(2)}) async-start(bf16[16,2,8192]{2,1,0:T(2,128)(2,1)} %reshape.76), calls=%async_computation.2 | async-start | bytes 1048576 | tf_op jit(solution)/shard_map/all_to_all | solution.py:51
  57.2 2.6 copy-start.4
  57.2 2.7 copy-start.18
  59.8 3.0 %copy-start.6 = (bf16[16,64,256]{2,1,0:T(8,128)(2,1)}, bf16[16,64,256]{2,1,0:T(8,128)(2,1)S(1)}, u32[]{:S(2)}) copy-start(bf16[16,64,256]{2,1,0:T(8,128)(2,1)S(1)} %get-tuple-element.22) | copy-start | bytes 1572868
  59.9 3.0 %copy-start.7 = (bf16[16,64,256]{2,1,0:T(8,128)(2,1)}, bf16[16,64,256]{2,1,0:T(8,128)(2,1)S(1)}, u32[]{:S(2)}) copy-start(bf16[16,64,256]{2,1,0:T(8,128)(2,1)S(1)} %pad_dynamic-slice_fusion.6) | copy-start | bytes 1572868
  61.3 1.5 copy-start.8
  61.4 1.5 copy-start.10
  62.9 1.5 copy-start.2
  64.4 7.2 %copy-start.12 = (bf16[16,64,256]{2,1,0:T(8,128)(2,1)}, bf16[16,64,256]{2,1,0:T(8,128)(2,1)S(1)}, u32[]{:S(2)}) copy-start(bf16[16,64,256]{2,1,0:T(8,128)(2,1)S(1)} %get-tuple-element.16) | copy-start | bytes 1572868
  64.4 20.2 %all-to-all-start.1 = ((bf16[16,64,256]{2,1,0:T(8,128)(2,1)}), bf16[16,64,256]{2,1,0:T(8,128)(2,1)S(1)}, u32[]{:S(2)}, u32[]{:S(2)}) async-start(bf16[16,64,256]{2,1,0:T(8,128)(2,1)} %get-tuple-element.17), calls=%async_computation.1 | async-start | bytes 1048576 | tf_op jit(solution)/shard_map/all_to_all | solution.py:43
  71.7 1.2 copy-start.19
  71.7 1.5 copy-start.24
  74.0 1.2 copy-start.23
  75.9 1.2 copy-start.21
  77.9 1.1 copy-start.9
  77.9 1.2 copy-start.11
  84.6 18.6 %all-to-all-start.3 = ((bf16[16,64,256]{2,1,0:T(8,128)(2,1)}), bf16[16,64,256]{2,1,0:T(8,128)(2,1)S(1)}, u32[]{:S(2)}, u32[]{:S(2)}) async-start(bf16[16,64,256]{2,1,0:T(8,128)(2,1)} %fusion.11), calls=%async_computation.3 | async-start | bytes 1048576 | tf_op jit(solution)/shard_map/all_to_all | solution.py:71
  88.7 62.3 %reduce-scatter.8.cloned.1.call-start = ((), (), s32[]{:S(2)}) async-start(), calls=%async_computation.8 | async-start | bytes 139264 | tf_op jit(solution)/shard_map/reduce_scatter | solution.py:77
  88.8 3.2 %copy-start.5 = (bf16[16,64,256]{2,1,0:T(8,128)(2,1)S(1)}, bf16[16,64,256]{2,1,0:T(8,128)(2,1)}, u32[]{:S(2)}) copy-start(bf16[16,64,256]{2,1,0:T(8,128)(2,1)} %copy-done.4) | copy-start | bytes 1572868
  88.8 3.2 %copy-start.22 = (f32[16,64,256]{2,1,0:T(8,128)S(1)}, f32[16,64,256]{2,1,0:T(8,128)}, u32[]{:S(2)}) copy-start(f32[16,64,256]{2,1,0:T(8,128)} %get-tuple-element.23) | copy-start | bytes 3145732
  91.9 11.2 %copy-start.1 = (bf16[1,1024,128]{2,1,0:T(8,128)(2,1)S(1)}, bf16[1,1024,128]{2,1,0:T(8,128)(2,1)}, u32[]{:S(2)}) copy-start(bf16[1,1024,128]{2,1,0:T(8,128)(2,1)} %param.8) | copy-start | bytes 786436
  93.4 10.9 %copy-start.3 = (bf16[16,64,256]{2,1,0:T(8,128)(2,1)S(1)}, bf16[16,64,256]{2,1,0:T(8,128)(2,1)}, u32[]{:S(2)}) copy-start(bf16[16,64,256]{2,1,0:T(8,128)(2,1)} %copy-done.2) | copy-start | bytes 1572868
  93.4 10.9 %copy-start.13 = (bf16[16,64,256]{2,1,0:T(8,128)(2,1)S(1)}, bf16[16,64,256]{2,1,0:T(8,128)(2,1)}, u32[]{:S(2)}) copy-start(bf16[16,64,256]{2,1,0:T(8,128)(2,1)} %copy-done.12) | copy-start | bytes 1572868
  94.5 114.7 %reduce-scatter.10.cloned.1.call-start = ((), (), s32[]{:S(2)}) async-start(), calls=%async_computation.9 | async-start | bytes 139264
  104.3 1.0 copy-start.14
  104.3 169.9 %reduce-scatter.6.cloned.1.call-start = ((), (), s32[]{:S(2)}) async-start(), calls=%async_computation.7 | async-start | bytes 2228224 | tf_op jit(solution)/shard_map/reduce_scatter | solution.py:70
  104.4 1.1 copy-start.15
  104.4 1.3 copy-start.16
Sparse Core Ops, SparseCore 0:
  94.6 56.3 reduce-scatter.7
  155.0 54.0 reduce-scatter.9
  213.5 60.6 reduce-scatter.5
where the time goes:
time: 282 us; the launch traced here: 281 us
  waiting for transfers between devices  187 us (66%)
  between operations  27.8 us (10%)
  matrix products  21.5 us (8%)
  starting transfers between devices  21.5 us (8%)
  local copies, waits for them, and re-layouts  11.4 us (4%)
  other arithmetic  11.1 us (4%)
    reduce_scatter x1, waiting for transfers between devices, shards(): lax.psum_scatter(stacked, 'tm', scatter_dimension=1, tiled=True)  65 us
    unnamed x4, waiting for transfers between devices  58.2 us
    reduce_scatter x1, waiting for transfers between devices, shards(): lax.psum_scatter(dec_term, 'tm', scatter_dimension=0, tiled=True)  42.8 us
    all_to_all x1, waiting for transfers between devices, shards(): lax.all_to_all(carried, 'tm', split_axis=0, concat_axis=1, tiled=True)  8.67 us
    all_to_all x1, waiting for transfers between devices, shards(): lax.all_to_all(start, 'tm', split_axis=1, concat_axis=0, tiled=True)  8.54 us
    unnamed x58, local copies, waits for them, and re-layouts  8.44 us
    unnamed x2, other arithmetic  7.66 us
    all_to_all x1, starting transfers between devices, shards(): lax.all_to_all(start, 'tm', split_axis=1, concat_axis=0, tiled=True)  7.4 us
  transfers between devices with their start and end apart: 7, of which 7 were waited for; matrix products, arithmetic and copies ran while one was open for 9% of the time, Pallas kernels for 0%

commit v1 on v0

--- a/solution.py
+++ b/solution.py
@@ -40,7 +40,8 @@
         )
         saved.append((joined, pre_act))
         latent = (latent.astype(jnp.float32) + jax.nn.silu(pre_act)).astype(jnp.bfloat16)
-    final = lax.all_to_all(latent, "tm", split_axis=0, concat_axis=1, tiled=True)
+    arr_out = lax.all_to_all(jnp.stack(jnp.split(latent, lax.axis_size("tm"), 0), 0), "tm", 0, 0)
+    final = jnp.concatenate(arr_out, 1)
     decoded = jnp.einsum(
         "fpd,dc->fpc", final, dec_weight, preferred_element_type=jnp.float32
     ).astype(jnp.bfloat16)

time: 282 us -> 292 us (1.035)
  local copies, waits for them, and re-layouts: 11.4 us -> 21.2 us
    unnamed x58 -> x73, local copies, waits for them, and re-layouts: 8.44 us -> 17.6 us
  transfers between devices with their start and end apart: 7 -> 7, of which waited for: 7 -> 7; matrix products, arithmetic and copies ran while one was open for 9% -> 8% of each run, Pallas kernels for 0% -> 0%
where the time goes in v1:
time: 292 us; the launch traced here: 291 us
  waiting for transfers between devices  187 us (64%)
  between operations  27.8 us (10%)
  matrix products  21.6 us (7%)
  starting transfers between devices  21.5 us (7%)
  local copies, waits for them, and re-layouts  21.2 us (7%)
  other arithmetic  11.1 us (4%)
    reduce_scatter x1, waiting for transfers between devices, shards(): lax.psum_scatter(stacked, 'tm', scatter_dimension=1, tiled=True)  64.9 us
    unnamed x4, waiting for transfers between devices  58.3 us
    reduce_scatter x1, waiting for transfers between devices, shards(): lax.psum_scatter(dec_term, 'tm', scatter_dimension=0, tiled=True)  42.8 us
    unnamed x73, local copies, waits for them, and re-layouts  17.6 us
    all_to_all x1, waiting for transfers between devices, shards(): lax.all_to_all(carried, 'tm', split_axis=0, concat_axis=1, tiled=True)  8.67 us
    all_to_all x1, waiting for transfers between devices, shards(): lax.all_to_all(start, 'tm', split_axis=1, concat_axis=0, tiled=True)  8.54 us
    unnamed x2, other arithmetic  7.66 us
    all_to_all x1, starting transfers between devices, shards(): lax.all_to_all(start, 'tm', split_axis=1, concat_axis=0, tiled=True)  7.4 us
  transfers between devices with their start and end apart: 7, of which 7 were waited for; matrix products, arithmetic and copies ran while one was open for 8% of the time, Pallas kernels for 0%

profile of v1, /device:TPU:0, one launch (start us, length us, event | category | flops | bytes accessed | tf_op | source)
XLA Modules:
  0.0 290.5 jit_solution(13496469032162262667)
XLA Ops:
  7.9 0.8 fusion.47
  8.7 1.2 fusion.2
  9.9 0.8 copy.26
  11.3 3.8 %reduce.1 = bf16[1024,256]{1,0:T(8,128)(2,1)S(1)} reduce(bf16[1024,1,256]{2,1,0:T(2,128)(2,1)S(1)} %bitcast.161, bf16[]{:T(256)} %broadcast.31), dimensions={1}, to_apply=%bitcast.156.reduce_sub_computation | reduce | bytes 1048578
  15.1 0.9 reshape.76
  16.0 7.4 %all-to-all-start = ((bf16[16,2,8192]{2,1,0:T(2,128)(2,1)}), bf16[16,2,8192]{2,1,0:T(2,128)(2,1)S(1)}, u32[]{:S(2)}, u32[]{:S(2)}) async-start(bf16[16,2,8192]{2,1,0:T(2,128)(2,1)} %reshape.76), calls=%async_computation | async-start | bytes 1048576 | tf_op jit(solution)/shard_map/all_to_all | solution.py:33
  23.8 0.8 copy.25
  24.6 3.8 %reduce = bf16[1024,256]{1,0:T(8,128)(2,1)S(1)} reduce(bf16[1024,1,256]{2,1,0:T(2,128)(2,1)S(1)} %bitcast.162, bf16[]{:T(256)} %broadcast.31), dimensions={1}, to_apply=%bitcast.155.reduce_sub_computation | reduce | bytes 1048578
  28.4 0.9 reshape.74
  29.4 8.5 %all-to-all-done = bf16[16,2,8192]{2,1,0:T(2,128)(2,1)S(1)} async-done(((bf16[16,2,8192]{2,1,0:T(2,128)(2,1)}), bf16[16,2,8192]{2,1,0:T(2,128)(2,1)S(1)}, u32[]{:S(2)}, u32[]{:S(2)}) %all-to-all-start) | async-done | bytes 524320 | tf_op jit(solution)/shard_map/all_to_all | solution.py:33
  37.9 4.1 %all-to-all-start.2 = ((bf16[16,2,8192]{2,1,0:T(2,128)(2,1)}), bf16[16,2,8192]{2,1,0:T(2,128)(2,1)S(1)}, u32[]{:S(2)}, u32[]{:S(2)}) async-start(bf16[16,2,8192]{2,1,0:T(2,128)(2,1)} %reshape.74), calls=%async_computation.2 | async-start | bytes 1048576 | tf_op jit(solution)/shard_map/all_to_all | solution.py:52
  57.2 2.6 add_convert_fusion.3
  59.9 1.4 add_convert_fusion.2
  61.4 1.4 add_convert_fusion.1
  62.9 1.5 multiply_convert_fusion
  65.0 0.6 constant_dynamic-update-slice_fusion.14
  65.6 0.6 constant_dynamic-update-slice_fusion.13
  66.9 0.6 constant_dynamic-update-slice_fusion.11
  67.5 0.6 constant_dynamic-update-slice_fusion.10
  68.7 0.6 constant_dynamic-update-slice_fusion.8
  69.3 0.6 constant_dynamic-update-slice_fusion.7
  69.9 0.6 constant_dynamic-update-slice_fusion.6
  70.5 0.6 constant_dynamic-update-slice_fusion.5
  71.2 0.6 constant_dynamic-update-slice_fusion.4
  72.4 0.6 constant_dynamic-update-slice_fusion.2
  73.0 0.6 constant_dynamic-update-slice_fusion.1
  74.2 5.7 %all-to-all-start.1 = ((bf16[16,1,64,256]{3,2,1,0:T(8,128)(2,1)}), bf16[16,1,64,256]{3,2,1,0:T(8,128)(2,1)S(1)}, u32[]{:S(2)}, u32[]{:S(2)}) async-start(bf16[16,1,64,256]{3,2,1,0:T(8,128)(2,1)} %constant_dynamic-update-slice_fusion), calls=%async_computation.1 | async-start | bytes 1048576 | tf_op jit(solution)/shard_map/all_to_all | solution.py:43
  80.0 1.4 fusion.25
  81.8 0.9 copy-done.19
  83.1 0.6 fusion.28
  84.1 0.9 copy-done.23
  85.0 0.6 fusion.31
  86.1 0.9 copy-done.21
  87.0 0.6 fusion.34
  87.8 1.1 fusion.11
  89.0 1.5 convolution_bitcast_fusion.1
  90.5 3.9 %all-to-all-done.1 = bf16[16,1,64,256]{3,2,1,0:T(8,128)(2,1)S(1)} async-done(((bf16[16,1,64,256]{3,2,1,0:T(8,128)(2,1)}), bf16[16,1,64,256]{3,2,1,0:T(8,128)(2,1)S(1)}, u32[]{:S(2)}, u32[]{:S(2)}) %all-to-all-start.1) | async-done | bytes 524320 | tf_op jit(solution)/shard_map/all_to_all | solution.py:43
  94.4 4.1 %all-to-all-start.3 = ((bf16[16,64,256]{2,1,0:T(8,128)(2,1)}), bf16[16,64,256]{2,1,0:T(8,128)(2,1)S(1)}, u32[]{:S(2)}, u32[]{:S(2)}) async-start(bf16[16,64,256]{2,1,0:T(8,128)(2,1)} %fusion.11), calls=%async_computation.3 | async-start | bytes 1048576 | tf_op jit(solution)/shard_map/all_to_all | solution.py:72
  98.6 3.1 %convolution_bitcast_fusion.2 = f32[1,512,256]{2,1,0:T(8,128)} fusion(bf16[16,64,256]{2,1,0:T(8,128)(2,1)} %copy-done.7, bf16[16,64,256]{2,1,0:T(8,128)(2,1)} %copy-done.6, bf16[16,64,256]{2,1,0:T(8,128)(2,1)S(1)} %fusion.7, f32[16,64,256]{2,1,0:T(8,128)} %get-tuple-element.25), kind=kOutput, calls=%fused_computation.18 | convolution fusion | flops 273154048 | bytes 3145728 | tf_op jit(solution)/shard_map/tpk,tpd->kd/dot_general | solution.py:60
  101.8 1.5 convolution_bitcast_fusion.3
  103.3 1.0 fusion.22
  104.3 8.7 %all-to-all-done.3 = bf16[16,64,256]{2,1,0:T(8,128)(2,1)S(1)} async-done(((bf16[16,64,256]{2,1,0:T(8,128)(2,1)}), bf16[16,64,256]{2,1,0:T(8,128)(2,1)S(1)}, u32[]{:S(2)}, u32[]{:S(2)}) %all-to-all-start.3) | async-done | bytes 524320 | tf_op jit(solution)/shard_map/all_to_all | solution.py:72
  113.4 0.8 copy.19
  115.5 1.5 pad_maximum_fusion
  117.1 1.0 fusion.3
  118.1 42.8 %reduce-scatter.8.cloned.1.call-done = f32[16,128]{1,0:T(8,128)} async-done(((f32[256,128]{1,0:T(8,128)}), f32[16,128]{1,0:T(8,128)}) %reduce-scatter.8.cloned.1.call-update) | async-done | bytes 8208 | tf_op jit(solution)/shard_map/reduce_scatter | solution.py:78
  160.8 58.2 %reduce-scatter.10.cloned.1.call-done = f32[8,256]{1,0:T(8,128)} async-done(((f32[128,256]{1,0:T(8,128)}), f32[8,256]{1,0:T(8,128)}) %reduce-scatter.10.cloned.1.call-update) | async-done | bytes 8208
  219.0 64.9 %reduce-scatter.6.cloned.1.call-done = f32[4,32,256]{2,1,0:T(8,128)} async-done(((f32[4,512,256]{2,1,0:T(8,128)}), f32[4,32,256]{2,1,0:T(8,128)}) %reduce-scatter.6.cloned.1.call-update) | async-done | bytes 131088 | tf_op jit(solution)/shard_map/reduce_scatter | solution.py:71
  (79 shorter events, 9.8 us)
Async XLA Ops:
  7.2 16.3 %copy-start = (bf16[1,1024,128]{2,1,0:T(8,128)(2,1)S(1)}, bf16[1,1024,128]{2,1,0:T(8,128)(2,1)}, u32[]{:S(2)}) copy-start(bf16[1,1024,128]{2,1,0:T(8,128)(2,1)} %param.15) | copy-start | bytes 786436
  10.7 12.7 %copy-start.17 = (bf16[256,128]{1,0:T(8,128)(2,1)S(1)}, bf16[256,128]{1,0:T(8,128)(2,1)}, u32[]{:S(2)}) copy-start(bf16[256,128]{1,0:T(8,128)(2,1)} %param.14) | copy-start | bytes 196612
  16.0 21.9 %all-to-all-start = ((bf16[16,2,8192]{2,1,0:T(2,128)(2,1)}), bf16[16,2,8192]{2,1,0:T(2,128)(2,1)S(1)}, u32[]{:S(2)}, u32[]{:S(2)}) async-start(bf16[16,2,8192]{2,1,0:T(2,128)(2,1)} %reshape.76), calls=%async_computation | async-start | bytes 1048576 | tf_op jit(solution)/shard_map/all_to_all | solution.py:33
  24.6 17.4 %copy-start.20 = (s32[4]{0:T(128)S(1)}, s32[4]{0:T(128)}, u32[]{:S(2)}) copy-start(s32[4]{0:T(128)} %param.10) | copy-start | bytes 52
  37.9 18.6 %all-to-all-start.2 = ((bf16[16,2,8192]{2,1,0:T(2,128)(2,1)}), bf16[16,2,8192]{2,1,0:T(2,128)(2,1)S(1)}, u32[]{:S(2)}, u32[]{:S(2)}) async-start(bf16[16,2,8192]{2,1,0:T(2,128)(2,1)} %reshape.74), calls=%async_computation.2 | async-start | bytes 1048576 | tf_op jit(solution)/shard_map/all_to_all | solution.py:52
  57.2 2.6 copy-start.4
  57.2 2.7 copy-start.18
  59.8 3.0 %copy-start.6 = (bf16[16,64,256]{2,1,0:T(8,128)(2,1)}, bf16[16,64,256]{2,1,0:T(8,128)(2,1)S(1)}, u32[]{:S(2)}) copy-start(bf16[16,64,256]{2,1,0:T(8,128)(2,1)S(1)} %get-tuple-element.22) | copy-start | bytes 1572868
  59.9 3.0 %copy-start.7 = (bf16[16,64,256]{2,1,0:T(8,128)(2,1)}, bf16[16,64,256]{2,1,0:T(8,128)(2,1)S(1)}, u32[]{:S(2)}) copy-start(bf16[16,64,256]{2,1,0:T(8,128)(2,1)S(1)} %pad_dynamic-slice_fusion.6) | copy-start | bytes 1572868
  61.3 1.5 copy-start.8
  61.4 1.5 copy-start.10
  62.9 1.5 copy-start.2
  64.4 15.6 %copy-start.12 = (bf16[16,64,256]{2,1,0:T(8,128)(2,1)S(1)}, bf16[16,64,256]{2,1,0:T(8,128)(2,1)}, u32[]{:S(2)}) copy-start(bf16[16,64,256]{2,1,0:T(8,128)(2,1)} %get-tuple-element.16) | copy-start | bytes 1572868
  74.2 20.2 %all-to-all-start.1 = ((bf16[16,1,64,256]{3,2,1,0:T(8,128)(2,1)}), bf16[16,1,64,256]{3,2,1,0:T(8,128)(2,1)S(1)}, u32[]{:S(2)}, u32[]{:S(2)}) async-start(bf16[16,1,64,256]{3,2,1,0:T(8,128)(2,1)} %constant_dynamic-update-slice_fusion), calls=%async_computation.1 | async-start | bytes 1048576 | tf_op jit(solution)/shard_map/all_to_all | solution.py:43
  81.5 1.2 copy-start.19
  81.5 1.5 copy-start.24
  83.8 1.2 copy-start.23
  85.8 1.2 copy-start.21
  87.8 1.1 copy-start.9
  87.8 1.2 copy-start.11
  94.4 18.6 %all-to-all-start.3 = ((bf16[16,64,256]{2,1,0:T(8,128)(2,1)}), bf16[16,64,256]{2,1,0:T(8,128)(2,1)S(1)}, u32[]{:S(2)}, u32[]{:S(2)}) async-start(bf16[16,64,256]{2,1,0:T(8,128)(2,1)} %fusion.11), calls=%async_computation.3 | async-start | bytes 1048576 | tf_op jit(solution)/shard_map/all_to_all | solution.py:72
  98.5 62.3 %reduce-scatter.8.cloned.1.call-start = ((), (), s32[]{:S(2)}) async-start(), calls=%async_computation.8 | async-start | bytes 139264 | tf_op jit(solution)/shard_map/reduce_scatter | solution.py:78
  98.6 3.2 %copy-start.5 = (bf16[16,64,256]{2,1,0:T(8,128)(2,1)S(1)}, bf16[16,64,256]{2,1,0:T(8,128)(2,1)}, u32[]{:S(2)}) copy-start(bf16[16,64,256]{2,1,0:T(8,128)(2,1)} %copy-done.4) | copy-start | bytes 1572868
  98.6 3.2 %copy-start.22 = (f32[16,64,256]{2,1,0:T(8,128)S(1)}, f32[16,64,256]{2,1,0:T(8,128)}, u32[]{:S(2)}) copy-start(f32[16,64,256]{2,1,0:T(8,128)} %get-tuple-element.23) | copy-start | bytes 3145732
  101.8 11.2 %copy-start.1 = (bf16[1,1024,128]{2,1,0:T(8,128)(2,1)S(1)}, bf16[1,1024,128]{2,1,0:T(8,128)(2,1)}, u32[]{:S(2)}) copy-start(bf16[1,1024,128]{2,1,0:T(8,128)(2,1)} %param.8) | copy-start | bytes 786436
  103.3 10.9 %copy-start.3 = (bf16[16,64,256]{2,1,0:T(8,128)(2,1)S(1)}, bf16[16,64,256]{2,1,0:T(8,128)(2,1)}, u32[]{:S(2)}) copy-start(bf16[16,64,256]{2,1,0:T(8,128)(2,1)} %copy-done.2) | copy-start | bytes 1572868
  103.3 10.9 %copy-start.13 = (bf16[16,64,256]{2,1,0:T(8,128)(2,1)S(1)}, bf16[16,64,256]{2,1,0:T(8,128)(2,1)}, u32[]{:S(2)}) copy-start(bf16[16,64,256]{2,1,0:T(8,128)(2,1)} %get-tuple-element.16) | copy-start | bytes 1572868
  104.3 114.8 %reduce-scatter.10.cloned.1.call-start = ((), (), s32[]{:S(2)}) async-start(), calls=%async_computation.9 | async-start | bytes 139264
  114.1 1.0 copy-start.14
  114.1 169.8 %reduce-scatter.6.cloned.1.call-start = ((), (), s32[]{:S(2)}) async-start(), calls=%async_computation.7 | async-start | bytes 2228224 | tf_op jit(solution)/shard_map/reduce_scatter | solution.py:71
  114.2 1.1 copy-start.15
  114.2 1.3 copy-start.16
Sparse Core Ops, SparseCore 0:
  104.4 56.3 reduce-scatter.7
  164.9 54.1 reduce-scatter.9
  223.4 60.5 reduce-scatter.5
